TPU v7x, 128 devices: a whole 4x4x4 slice. The times are simulated.
128 devices in a mesh: dom: 8 (over z, core), grp: 16 (over x, y).
Axes of the slice: x: 4, y: 4, z: 4, core: 2. Of those that a mesh axis runs over, the one named last changes fastest.
Arguments:
- inputs: bfloat16 [393216, 256], P(('dom', 'grp')), may hold values from -6 to 6
- initial: bfloat16 [393216, 256], P(('dom', 'grp')), may hold values from -6 to 6
- history: bfloat16 [393216, 256], P(('dom', 'grp')), may hold values from -6 to 6
- upstream: bfloat16 [393216, 256], P(('dom', 'grp')), may hold values from -6 to 6
- weight: bfloat16 [256, 256], replicated, may hold values from -0.375 to 0.375
- tile_vals: bfloat16 [36864, 128, 128], P(('dom', 'grp')), may hold values from 0 to 0.088378906
- tile_row: int32 [36864], P(('dom', 'grp')), may hold values from 0 to 23
- tile_col: int32 [36864], P(('dom', 'grp')), may hold values from 0 to 47, as said below
- tile_count: int32 [128], P(('dom', 'grp')), may hold values from 48 to 288, as said below
- send_rows: int32 [8, 16, 128, 8], P('dom', 'grp'), may hold values from 0 to 3071
- cache_ask: int32 [8, 16, 8, 2], P('dom', 'grp'), may hold values from 0 to 23
Outputs:
- layer_out: bfloat16 [393216, 256], P(('dom', 'grp'))
- grad_inputs: float32 [393216, 256], P(('dom', 'grp'))
- grad_weight: float32 [256, 256], replicated
Inputs may be any that keep to these rules, and one draw needn't show every extreme that they name: `send_rows`: row numbers within the sending section. `cache_ask`: block numbers within the owning section. `tile_row`: row block within the section. `tile_col`: in each section's list the first 48 tiles name every column block once. `tile_count`: some section has exactly 288 live tiles.
All inputs are finite; a program needn't handle non-finite values.
Results may differ from a plain program's by a relative error of at most 0.0053.
Values may be sent and summed in bfloat16 or wider, within the bound.
A program may use at most 128 MiB of HBM per device.

v0:
```python
import math
import jax
import jax.numpy as jnp
from jax import lax
from jax.sharding import PartitionSpec as P

alpha_res = 0.1
beta_map = 0.4


def silu_slope(pre_act):
    squash = jax.nn.sigmoid(pre_act)
    return squash * (1.0 + pre_act * (1.0 - squash))


def turn_width(slot_count):
    for option_width in (96, 48, 32, 16, 8):
        return option_width
    return slot_count


def per_device(
    inputs,
    initial,
    history,
    upstream,
    weight,
    tile_vals,
    tile_row,
    tile_col,
    tile_count,
    send_rows,
    cache_ask,
):
    row_count, feature_dim = inputs.shape
    block_rows = tile_vals.shape[1]
    block_count = row_count // block_rows
    slot_count = tile_vals.shape[0]
    group_size = turn_width(slot_count)
    dom_count = lax.axis_size("dom")
    grp_count = lax.axis_size("grp")
    peer_count = dom_count * grp_count
    send_list = send_rows.reshape(peer_count, -1)
    per_peer = send_list.shape[1]
    ask_list = cache_ask.reshape(dom_count, -1)
    asked_per = ask_list.shape[1]
    outgoing = inputs[send_list.reshape(-1)].reshape(peer_count, per_peer, feature_dim)
    arrived = lax.all_to_all(outgoing, ("dom", "grp"), split_axis=0, concat_axis=0, tiled=True)
    arrived = arrived.reshape(peer_count * per_peer, feature_dim)
    wanted = lax.all_to_all(ask_list, "dom", split_axis=0, concat_axis=0, tiled=True)
    own_blocks = history.reshape(block_count, block_rows, feature_dim)
    served = own_blocks[wanted.reshape(-1)].reshape(dom_count, asked_per * block_rows, feature_dim)
    cached = lax.all_to_all(served, "dom", split_axis=0, concat_axis=0, tiled=True)
    cached = cached.reshape(dom_count * asked_per * block_rows, feature_dim)
    columns = jnp.concatenate([inputs, arrived, cached], axis=0)
    col_blocks = columns.reshape(-1, block_rows, feature_dim)
    column_total = col_blocks.shape[0]
    live_count = tile_count[0]
    turn_count = (live_count + group_size - 1) // group_size

    def turn_slices(turn_index):
        offset = turn_index * group_size
        tile_block = lax.dynamic_slice_in_dim(tile_vals, offset, group_size, 0)
        row_pick = lax.dynamic_slice_in_dim(tile_row, offset, group_size, 0)
        col_pick = lax.dynamic_slice_in_dim(tile_col, offset, group_size, 0)
        live_part = (offset + jnp.arange(group_size) < live_count).astype(jnp.float32)
        return (tile_block, row_pick, col_pick, live_part)

    def forward_turn(turn_index, totals):
        tile_block, row_pick, col_pick, live_part = turn_slices(turn_index)
        products = jnp.einsum(
            "tij,tjd->tid", tile_block, col_blocks[col_pick], preferred_element_type=jnp.float32
        )
        placing = (row_pick[:, None] == jnp.arange(block_count)[None, :]).astype(
            jnp.float32
        ) * live_part[:, None]
        return totals + jnp.einsum(
            "tr,tid->rid", placing, products, precision=lax.Precision.HIGHEST
        )

    gathered = lax.fori_loop(
        0, turn_count, forward_turn, jnp.zeros((block_count, block_rows, feature_dim), jnp.float32)
    )
    mixture = (1.0 - alpha_res) * gathered.reshape(
        row_count, feature_dim
    ) + alpha_res * initial.astype(jnp.float32)
    mixed_b = mixture.astype(jnp.bfloat16)
    pre_act = (1.0 - beta_map) * mixture + beta_map * jnp.dot(
        mixed_b, weight, preferred_element_type=jnp.float32
    )
    layer_out = jax.nn.silu(pre_act).astype(jnp.bfloat16)
    act_slope = upstream.astype(jnp.float32) * silu_slope(pre_act)
    slope_b = act_slope.astype(jnp.bfloat16)
    weight_part = lax.dot_general(
        mixed_b, slope_b, (((0,), (0,)), ((), ())), preferred_element_type=jnp.float32
    )
    through_weight = lax.dot_general(
        slope_b, weight, (((1,), (1,)), ((), ())), preferred_element_type=jnp.float32
    )
    back_grad = (
        (1.0 - alpha_res) * ((1.0 - beta_map) * act_slope + beta_map * through_weight)
    ).astype(jnp.bfloat16)
    back_blocks = back_grad.reshape(block_count, block_rows, feature_dim)

    def backward_turn(turn_index, totals):
        tile_block, row_pick, col_pick, live_part = turn_slices(turn_index)
        spread = jnp.einsum(
            "tji,tjd->tid", tile_block, back_blocks[row_pick], preferred_element_type=jnp.float32
        )
        onto_mask = (col_pick[:, None] == jnp.arange(column_total)[None, :]).astype(
            jnp.float32
        ) * live_part[:, None]
        return totals + jnp.einsum(
            "tc,tid->cid", onto_mask, spread, precision=lax.Precision.HIGHEST
        )

    column_grads = lax.fori_loop(
        0,
        turn_count,
        backward_turn,
        jnp.zeros((column_total, block_rows, feature_dim), jnp.float32),
    )
    fresh_blocks = peer_count * per_peer // block_rows
    own_grads = column_grads[:block_count].reshape(row_count, feature_dim)
    fresh_grads = (
        column_grads[block_count : block_count + fresh_blocks]
        .reshape(peer_count, per_peer, feature_dim)
        .astype(jnp.bfloat16)
    )
    returned = lax.all_to_all(fresh_grads, ("dom", "grp"), split_axis=0, concat_axis=0, tiled=True)
    returned = returned.reshape(peer_count * per_peer, feature_dim).astype(jnp.float32)
    grad_inputs = own_grads.at[send_list.reshape(-1)].add(returned)
    weight_total = lax.psum(weight_part, ("dom", "grp"))
    grad_weight = weight_total * (beta_map / math.sqrt(row_count * peer_count))
    return (layer_out, grad_inputs, grad_weight)


def solution(mesh):
    placed = (
        P(("dom", "grp"), None),
        P(("dom", "grp"), None),
        P(("dom", "grp"), None),
        P(("dom", "grp"), None),
        P(),
        P(("dom", "grp"), None, None),
        P(("dom", "grp")),
        P(("dom", "grp")),
        P(("dom", "grp")),
        P("dom", "grp", None, None),
        P("dom", "grp", None, None),
    )
    return jax.shard_map(
        per_device,
        mesh=mesh,
        in_specs=placed,
        out_specs=(P(("dom", "grp"), None), P(("dom", "grp"), None), P()),
        check_vma=False,
    )
```

profile of v0, /device:TPU:1, one launch (start us, length us, event | category | flops | bytes accessed | tf_op | source)
XLA Modules:
  0.0 450.1 jit_solution(1641534458222594287)
XLA Ops:
  8.6 6.8 %all-to-all-start.1 = ((s32[8,1,2]{2,1,0:T(1,128)}), s32[8,1,2]{2,1,0:T(1,128)S(1)}, u32[]{:S(2)}, u32[]{:S(2)}) async-start(s32[8,1,2]{2,1,0:T(1,128)} %copy.25), calls=%async_computation.1 | async-start | bytes 8192 | tf_op jit(solution)/shard_map/all_to_all | solution.py:50
  17.0 6.2 %gather_fusion.2 = bf16[1024,256]{1,0:T(8,128)(2,1)} fusion(bf16[3072,256]{1,0:T(8,128)(2,1)} %param.15, s32[1024]{0:T(1024)S(1)} %broadcast_clamp_fusion), kind=kCustom, calls=%fused_computation.2 | custom fusion | bytes 1052672 | tf_op jit(solution)/shard_map/gather | solution.py:47
  23.2 9.9 %all-to-all-start = ((bf16[128,8,256]{2,1,0:T(8,128)(2,1)}), bf16[128,8,256]{2,1,0:T(8,128)(2,1)}, u32[]{:S(2)}, u32[]{:S(2)}) async-start(bf16[128,8,256]{2,1,0:T(8,128)(2,1)} %bitcast.49), calls=%async_computation | async-start | bytes 1048576 | tf_op jit(solution)/shard_map/all_to_all | solution.py:48
  36.0 10.1 %all-to-all-done = bf16[128,8,256]{2,1,0:T(8,128)(2,1)} async-done(((bf16[128,8,256]{2,1,0:T(8,128)(2,1)}), bf16[128,8,256]{2,1,0:T(8,128)(2,1)}, u32[]{:S(2)}, u32[]{:S(2)}) %all-to-all-start) | async-done | bytes 524320 | tf_op jit(solution)/shard_map/all_to_all | solution.py:48
  46.1 4.8 %all-to-all-start.2 = ((bf16[8,256,256]{2,1,0:T(8,128)(2,1)}), bf16[8,256,256]{2,1,0:T(8,128)(2,1)S(1)}, u32[]{:S(2)}, u32[]{:S(2)}) async-start(bf16[8,256,256]{2,1,0:T(8,128)(2,1)} %bitcast.46), calls=%async_computation.2 | async-start | bytes 2097152 | tf_op jit(solution)/shard_map/all_to_all | solution.py:53
  51.6 14.4 %all-to-all-done.2 = bf16[8,256,256]{2,1,0:T(8,128)(2,1)S(1)} async-done(((bf16[8,256,256]{2,1,0:T(8,128)(2,1)}), bf16[8,256,256]{2,1,0:T(8,128)(2,1)S(1)}, u32[]{:S(2)}, u32[]{:S(2)}) %all-to-all-start.2) | async-done | bytes 1048608 | tf_op jit(solution)/shard_map/all_to_all | solution.py:53
  66.0 10.3 %pad_maximum_fusion = bf16[6144,256]{1,0:T(8,128)(2,1)} fusion(bf16[2048,256]{1,0:T(8,128)(2,1)S(1)} %bitcast.47, bf16[1024,256]{1,0:T(8,128)(2,1)} %bitcast.5, bf16[3072,256]{1,0:T(8,128)(2,1)S(1)} %copy-done.6), kind=kLoop, calls=%fused_computation.43 | loop fusion | flops 9437184 | bytes 6291456 | tf_op jit(solution)/shard_map/concatenate | solution.py:55
  78.2 30.3 %while.20 = (s32[]{:T(128)}, f32[24,128,256]{2,0,1:T(8,128)}, s32[]{:T(128)}, s32[288]{0:T(512)S(1)}, s32[]{:T(128)}, /*index=5*/bf16[288,128,128]{2,1,0:T(8,128...) while((s32[]{:T(128)}, f32[24,128,256]{2,0,1:T(8,128)}, ...), condition=%wide.region_1.2_spmd, body=%wide.region_0.1_spmd.sunk | while | flops 1712068736 | bytes 78650992 | solution.py:81
  79.2 7.9 %gather_fusion = bf16[96,128,256]{2,1,0:T(8,128)(2,1)} fusion(bf16[48,128,256]{2,1,0:T(8,128)(2,1)} %get-tuple-element.264, s32[1024]{0:T(1024)S(1)} %pad_clamp_fusion.5), kind=kCustom, calls=%fused_computation.clone.1 | custom fusion | bytes 12583296 | tf_op jit(solution)/shard_map/while/body/gather | solution.py:72
  87.1 5.7 %fusion.61 = f32[96,128,256]{2,1,0:T(8,128)S(1)} fusion(bf16[96,128,256]{2,1,0:T(8,128)(2,1)} %gather_fusion, bf16[288,128,128]{2,1,0:T(8,128)(2,1)} %get-tuple-element.262, s32[]{:T(128)S(6)} %select_n.56), kind=kOutput, calls=%fused_computation.7.clone.1 | convolution fusion | flops 805306368 | bytes 22020100 | tf_op jit(solution)/shard_map/while/body/tij,tjd->tid/dot_general | solution.py:71
  92.8 13.7 %fusion.62 = f32[24,128,256]{2,0,1:T(8,128)S(1)} fusion(f32[24,128,256]{2,0,1:T(8,128)S(1)} %copy-done.4, f32[96,128,256]{2,1,0:T(8,128)S(1)} %fusion.61, f32[96]{0:T(128)S(1)} %compare_convert_fusion.4, s32[96]{0:T(128)S(1)} %dynamic_slice.32), kind=kOutput, calls=%fused_computation.9.clone.1 | convolution fusion | flops 906760704 | bytes 18875136 | tf_op jit(solution)/shard_map/while/body/tr,tid->rid/dot_general | solution.py:77
  115.5 2.9 fusion.31
  118.5 3.5 broadcast_in_dim.13
  122.0 30.3 %while.21 = (s32[]{:T(128)}, f32[48,128,256]{2,0,1:T(8,128)}, s32[]{:T(128)}, s32[288]{0:T(512)S(1)}, s32[]{:T(128)}, /*index=5*/bf16[288,128,128]{2,1,0:T(8,128...) while((s32[]{:T(128)}, f32[48,128,256]{2,0,1:T(8,128)}, ...), condition=%wide.region_3.4_spmd, body=%wide.region_2.3_spmd.sunk | while | flops 2618829312 | bytes 110108272 | solution.py:117
  122.9 5.9 %gather_fusion.1 = bf16[96,128,256]{2,1,0:T(8,128)(2,1)} fusion(bf16[24,128,256]{2,1,0:T(8,128)(2,1)S(1)} %get-tuple-element.300, s32[1024]{0:T(1024)S(1)} %pad_clamp_fusion.6), kind=kCustom, calls=%fused_computation.1.clone.1 | custom fusion | bytes 12583296 | tf_op jit(solution)/shard_map/while/body/gather | solution.py:108
  128.9 5.7 %fusion.67 = f32[96,128,256]{2,1,0:T(8,128)S(1)} fusion(bf16[96,128,256]{2,1,0:T(8,128)(2,1)} %gather_fusion.1, bf16[288,128,128]{2,1,0:T(8,128)(2,1)} %get-tuple-element.298, s32[]{:T(128)S(6)} %select_n.58), kind=kOutput, calls=%fused_computation.23.clone.1 | convolution fusion | flops 805306368 | bytes 22020100 | tf_op jit(solution)/shard_map/while/body/tji,tjd->tid/dot_general | solution.py:107
  134.6 14.8 %fusion.68 = f32[48,128,256]{2,0,1:T(8,128)S(1)} fusion(f32[48,128,256]{2,0,1:T(8,128)S(1)} %copy-done.2, f32[96,128,256]{2,1,0:T(8,128)S(1)} %fusion.67, f32[96]{0:T(128)S(1)} %compare_convert_fusion.5, s32[96]{0:T(128)S(1)} %dynamic_slice.35), kind=kOutput, calls=%fused_computation.25.clone.1 | convolution fusion | flops 1813521408 | bytes 25166592 | tf_op jit(solution)/shard_map/while/body/tc,tid->cid/dot_general | solution.py:113
  149.4 2.7 copy-done.3
  152.3 6.2 %copy.29 = bf16[48,128,256]{2,1,0:T(8,128)(2,1)S(1)} copy(f32[48,128,256]{2,0,1:T(8,128)} %get-tuple-element.90) | data formatting | bytes 9437184 | tf_op jit(solution)/shard_map/while | solution.py:117
  159.3 123.0 %all-to-all-start.3 = ((bf16[128,8,256]{2,1,0:T(8,128)(2,1)}), bf16[128,8,256]{2,1,0:T(8,128)(2,1)S(1)}, u32[]{:S(2)}, u32[]{:S(2)}) async-start(bf16[128,8,256]{2,1,0:T(8,128)(2,1)} %bitcast.15), calls=%async_computation.3 | async-start | bytes 1048576 | tf_op jit(solution)/shard_map/all_to_all | solution.py:130
  282.4 5.0 %fusion.34 = f32[256,256]{1,0:T(8,128)} fusion(f32[3072,256]{1,0:T(8,128)} %copy-done.7, f32[3072,256]{1,0:T(8,128)} %copy-done.15, bf16[3072,256]{1,0:T(8,128)(2,1)S(1)} %copy-done.11), kind=kOutput, calls=%fused_computation.52 | convolution fusion | flops 411303936 | bytes 8126464 | tf_op jit(solution)/shard_map/dot_general | solution.py:94
  289.6 2.6 copy.28
  292.2 139.4 %all-reduce.2.cloned.1.call-done = f32[256,256]{1,0:T(8,128)} async-done(((f32[256,256]{1,0:T(8,128)}), f32[256,256]{1,0:T(8,128)}) %all-reduce.2.cloned.1.call-update) | async-done | bytes 262160 | tf_op jit(solution)/shard_map/psum | solution.py:133
  433.3 9.7 %scatter_custom_fusion = f32[3072,256]{1,0:T(8,128)} fusion(f32[3072,256]{1,0:T(8,128)} %bitcast.48, s32[1024]{0:T(1024)} %bitcast.51, bf16[128,8,256]{2,1,0:T(8,128)(2,1)S(1)} %all-to-all-done.3), kind=kCustom, calls=%fused_computation.50 | custom fusion | flops 524288 | bytes 3670016 | tf_op jit(solution)/shard_map/scatter-add | solution.py:132
  (62 shorter events, 22.7 us)
Async XLA Ops:
  7.2 27.2 %copy-start = (bf16[3072,256]{1,0:T(8,128)(2,1)S(1)}, bf16[3072,256]{1,0:T(8,128)(2,1)}, u32[]{:S(2)}) copy-start(bf16[3072,256]{1,0:T(8,128)(2,1)} %param.17) | copy-start | bytes 4718596
  8.6 14.5 %all-to-all-start.1 = ((s32[8,1,2]{2,1,0:T(1,128)}), s32[8,1,2]{2,1,0:T(1,128)S(1)}, u32[]{:S(2)}, u32[]{:S(2)}) async-start(s32[8,1,2]{2,1,0:T(1,128)} %copy.25), calls=%async_computation.1 | async-start | bytes 8192 | tf_op jit(solution)/shard_map/all_to_all | solution.py:50
  16.4 0.6 copy-start.9
  23.2 42.9 %copy-start.6 = (bf16[3072,256]{1,0:T(8,128)(2,1)S(1)}, bf16[3072,256]{1,0:T(8,128)(2,1)}, u32[]{:S(2)}) copy-start(bf16[3072,256]{1,0:T(8,128)(2,1)} %param.15) | copy-start | bytes 4718596
  23.2 22.9 %all-to-all-start = ((bf16[128,8,256]{2,1,0:T(8,128)(2,1)}), bf16[128,8,256]{2,1,0:T(8,128)(2,1)}, u32[]{:S(2)}, u32[]{:S(2)}) async-start(bf16[128,8,256]{2,1,0:T(8,128)(2,1)} %bitcast.49), calls=%async_computation | async-start | bytes 1048576 | tf_op jit(solution)/shard_map/all_to_all | solution.py:48
  46.1 19.9 %all-to-all-start.2 = ((bf16[8,256,256]{2,1,0:T(8,128)(2,1)}), bf16[8,256,256]{2,1,0:T(8,128)(2,1)S(1)}, u32[]{:S(2)}, u32[]{:S(2)}) async-start(bf16[8,256,256]{2,1,0:T(8,128)(2,1)} %bitcast.46), calls=%async_computation.2 | async-start | bytes 2097152 | tf_op jit(solution)/shard_map/all_to_all | solution.py:53
  76.3 1.9 copy-start.13
  76.3 1.9 copy-start.14
  87.1 5.7 %copy-start.4 = (f32[24,128,256]{2,0,1:T(8,128)S(1)}, f32[24,128,256]{2,0,1:T(8,128)}, u32[]{:S(2)}) copy-start(f32[24,128,256]{2,0,1:T(8,128)} %get-tuple-element.246) | copy-start | bytes 9437188 | tf_op jit(solution)/shard_map/while
  106.5 1.7 copy-start.5
  110.7 1.4 copy-start.8
  112.1 0.9 copy-start.12
  113.0 2.3 copy-start.7
  113.0 2.5 copy-start.10
  115.3 3.2 copy-start.15
  128.9 5.7 %copy-start.2 = (f32[48,128,256]{2,0,1:T(8,128)S(1)}, f32[48,128,256]{2,0,1:T(8,128)}, u32[]{:S(2)}) copy-start(f32[48,128,256]{2,0,1:T(8,128)} %get-tuple-element.282) | copy-start | bytes 18874372 | tf_op jit(solution)/shard_map/while
  149.4 2.7 copy-start.3
  152.2 130.1 %copy-start.11 = (bf16[3072,256]{1,0:T(8,128)(2,1)S(1)}, bf16[3072,256]{1,0:T(8,128)(2,1)}, u32[]{:S(2)}) copy-start(bf16[3072,256]{1,0:T(8,128)(2,1)} %param.18) | copy-start | bytes 4718596
  159.3 273.9 %all-to-all-start.3 = ((bf16[128,8,256]{2,1,0:T(8,128)(2,1)}), bf16[128,8,256]{2,1,0:T(8,128)(2,1)S(1)}, u32[]{:S(2)}, u32[]{:S(2)}) async-start(bf16[128,8,256]{2,1,0:T(8,128)(2,1)} %bitcast.15), calls=%async_computation.3 | async-start | bytes 1048576 | tf_op jit(solution)/shard_map/all_to_all | solution.py:130
  282.3 149.3 %all-reduce.2.cloned.1.call-start = ((), (), s32[]{:S(2)}) async-start(), calls=%async_computation.4 | async-start | bytes 524288 | tf_op jit(solution)/shard_map/psum | solution.py:133
  289.5 153.5 %copy-start.1 = (bf16[3072,256]{1,0:T(8,128)(2,1)S(1)}, bf16[3072,256]{1,0:T(8,128)(2,1)}, u32[]{:S(2)}) copy-start(bf16[3072,256]{1,0:T(8,128)(2,1)} %param.17) | copy-start | bytes 4718596
Sparse Core Ops, SparseCore 0:
  288.5 143.0 all-reduce.1
where the time goes:
time: 456 us; the launch traced here: 450 us
  waiting for transfers between devices  164 us (36%)
  starting transfers between devices  145 us (32%)
  matrix products  50.1 us (11%)
  local copies, waits for them, and re-layouts  48.9 us (11%)
  other arithmetic  26.4 us (6%)
  between operations  15.1 us (3%)
    psum x1, waiting for transfers between devices, per_device(): weight_total = lax.psum(weight_part, ('dom', 'grp'))  139 us
    all_to_all x1, starting transfers between devices, per_device(): lax.all_to_all(fresh_grads, ('dom', 'grp'), split_axis=0, concat_axis=0,...  123 us
    dot_general x1, matrix products, backward_turn(): jnp.einsum('tc,tid->cid', onto_mask, spread, precision=lax.Precision.HIGH...  14.8 us
    all_to_all x1, waiting for transfers between devices, per_device(): lax.all_to_all(served, 'dom', split_axis=0, concat_axis=0, tiled=True)  14.4 us
    dot_general x1, matrix products, forward_turn(): jnp.einsum('tr,tid->rid', placing, products, precision=lax.Precision.HIGH...  13.7 us
    concatenate x1, other arithmetic, per_device(): columns = jnp.concatenate([inputs, arrived, cached], axis=0)  10.3 us
    all_to_all x1, waiting for transfers between devices, per_device(): lax.all_to_all(outgoing, ('dom', 'grp'), split_axis=0, concat_axis=0, til...  10.1 us
    all_to_all x1, starting transfers between devices, per_device(): lax.all_to_all(outgoing, ('dom', 'grp'), split_axis=0, concat_axis=0, til...  9.95 us
  transfers between devices with their start and end apart: 5, of which 3 were waited for; matrix products, arithmetic and copies ran while one was open for 5% of the time, Pallas kernels for 0%

commit v1 on v0

--- a/solution.py
+++ b/solution.py
@@ -130,7 +130,7 @@
     returned = lax.all_to_all(fresh_grads, ("dom", "grp"), split_axis=0, concat_axis=0, tiled=True)
     returned = returned.reshape(peer_count * per_peer, feature_dim).astype(jnp.float32)
     grad_inputs = own_grads.at[send_list.reshape(-1)].add(returned)
-    weight_total = lax.psum(weight_part, ("dom", "grp"))
+    weight_total = lax.psum(lax.psum(weight_part, "dom"), "grp")
     grad_weight = weight_total * (beta_map / math.sqrt(row_count * peer_count))
     return (layer_out, grad_inputs, grad_weight)
 

time: 456 us -> 402 us (0.88)
  waiting for transfers between devices: 164 us -> 108 us
    psum x1 -> x2, waiting for transfers between devices: 139 us -> 83 us  [per_device(): weight_total = lax.psum(lax.psum(weight_part, 'dom'), 'grp')]
  transfers between devices with their start and end apart: 5 -> 6, of which waited for: 3 -> 3; matrix products, arithmetic and copies ran while one was open for 5% -> 14% of each run, Pallas kernels for 0% -> 0%
where the time goes in v1:
time: 402 us; the launch traced here: 396 us
  starting transfers between devices  145 us (36%)
  waiting for transfers between devices  108 us (27%)
  local copies, waits for them, and re-layouts  50.3 us (13%)
  matrix products  49.9 us (12%)
  other arithmetic  26.4 us (7%)
  between operations  15.1 us (4%)
    all_to_all x1, starting transfers between devices, per_device(): lax.all_to_all(fresh_grads, ('dom', 'grp'), split_axis=0, concat_axis=0,...  123 us
    psum x2, waiting for transfers between devices, per_device(): weight_total = lax.psum(lax.psum(weight_part, 'dom'), 'grp')  83 us
    dot_general x1, matrix products, backward_turn(): jnp.einsum('tc,tid->cid', onto_mask, spread, precision=lax.Precision.HIGH...  14.8 us
    all_to_all x1, waiting for transfers between devices, per_device(): lax.all_to_all(served, 'dom', split_axis=0, concat_axis=0, tiled=True)  14.4 us
    dot_general x1, matrix products, forward_turn(): jnp.einsum('tr,tid->rid', placing, products, precision=lax.Precision.HIGH...  13.7 us
    concatenate x1, other arithmetic, per_device(): columns = jnp.concatenate([inputs, arrived, cached], axis=0)  10.3 us
    all_to_all x1, waiting for transfers between devices, per_device(): lax.all_to_all(outgoing, ('dom', 'grp'), split_axis=0, concat_axis=0, til...  10.1 us
    all_to_all x1, starting transfers between devices, per_device(): lax.all_to_all(outgoing, ('dom', 'grp'), split_axis=0, concat_axis=0, til...  9.95 us
  transfers between devices with their start and end apart: 6, of which 3 were waited for; matrix products, arithmetic and copies ran while one was open for 14% of the time, Pallas kernels for 0%

profile of v1, /device:TPU:1, one launch (start us, length us, event | category | flops | bytes accessed | tf_op | source)
XLA Modules:
  0.0 395.8 jit_solution(10505469015950495526)
XLA Ops:
  8.6 6.8 %all-to-all-start.1 = ((s32[8,1,2]{2,1,0:T(1,128)}), s32[8,1,2]{2,1,0:T(1,128)S(1)}, u32[]{:S(2)}, u32[]{:S(2)}) async-start(s32[8,1,2]{2,1,0:T(1,128)} %copy.25), calls=%async_computation.1 | async-start | bytes 8192 | tf_op jit(solution)/shard_map/all_to_all | solution.py:50
  17.0 6.2 %gather_fusion.2 = bf16[1024,256]{1,0:T(8,128)(2,1)} fusion(bf16[3072,256]{1,0:T(8,128)(2,1)} %param.15, s32[1024]{0:T(1024)S(1)} %broadcast_clamp_fusion), kind=kCustom, calls=%fused_computation.2 | custom fusion | bytes 1052672 | tf_op jit(solution)/shard_map/gather | solution.py:47
  23.2 9.9 %all-to-all-start = ((bf16[128,8,256]{2,1,0:T(8,128)(2,1)}), bf16[128,8,256]{2,1,0:T(8,128)(2,1)}, u32[]{:S(2)}, u32[]{:S(2)}) async-start(bf16[128,8,256]{2,1,0:T(8,128)(2,1)} %bitcast.49), calls=%async_computation | async-start | bytes 1048576 | tf_op jit(solution)/shard_map/all_to_all | solution.py:48
  36.0 10.1 %all-to-all-done = bf16[128,8,256]{2,1,0:T(8,128)(2,1)} async-done(((bf16[128,8,256]{2,1,0:T(8,128)(2,1)}), bf16[128,8,256]{2,1,0:T(8,128)(2,1)}, u32[]{:S(2)}, u32[]{:S(2)}) %all-to-all-start) | async-done | bytes 524320 | tf_op jit(solution)/shard_map/all_to_all | solution.py:48
  46.1 4.8 %all-to-all-start.2 = ((bf16[8,256,256]{2,1,0:T(8,128)(2,1)}), bf16[8,256,256]{2,1,0:T(8,128)(2,1)S(1)}, u32[]{:S(2)}, u32[]{:S(2)}) async-start(bf16[8,256,256]{2,1,0:T(8,128)(2,1)} %bitcast.46), calls=%async_computation.2 | async-start | bytes 2097152 | tf_op jit(solution)/shard_map/all_to_all | solution.py:53
  51.6 14.4 %all-to-all-done.2 = bf16[8,256,256]{2,1,0:T(8,128)(2,1)S(1)} async-done(((bf16[8,256,256]{2,1,0:T(8,128)(2,1)}), bf16[8,256,256]{2,1,0:T(8,128)(2,1)S(1)}, u32[]{:S(2)}, u32[]{:S(2)}) %all-to-all-start.2) | async-done | bytes 1048608 | tf_op jit(solution)/shard_map/all_to_all | solution.py:53
  66.0 10.3 %pad_maximum_fusion = bf16[6144,256]{1,0:T(8,128)(2,1)} fusion(bf16[2048,256]{1,0:T(8,128)(2,1)S(1)} %bitcast.47, bf16[1024,256]{1,0:T(8,128)(2,1)} %bitcast.5, bf16[3072,256]{1,0:T(8,128)(2,1)S(1)} %copy-done.6), kind=kLoop, calls=%fused_computation.43 | loop fusion | flops 9437184 | bytes 6291456 | tf_op jit(solution)/shard_map/concatenate | solution.py:55
  78.2 30.3 %while.20 = (s32[]{:T(128)}, f32[24,128,256]{2,0,1:T(8,128)}, s32[]{:T(128)}, s32[288]{0:T(512)S(1)}, s32[]{:T(128)}, /*index=5*/bf16[288,128,128]{2,1,0:T(8,128...) while((s32[]{:T(128)}, f32[24,128,256]{2,0,1:T(8,128)}, ...), condition=%wide.region_1.2_spmd, body=%wide.region_0.1_spmd.sunk | while | flops 1712068736 | bytes 78650992 | solution.py:81
  79.2 7.9 %gather_fusion = bf16[96,128,256]{2,1,0:T(8,128)(2,1)} fusion(bf16[48,128,256]{2,1,0:T(8,128)(2,1)} %get-tuple-element.264, s32[1024]{0:T(1024)S(1)} %pad_clamp_fusion.5), kind=kCustom, calls=%fused_computation.clone.1 | custom fusion | bytes 12583296 | tf_op jit(solution)/shard_map/while/body/gather | solution.py:72
  87.1 5.7 %fusion.61 = f32[96,128,256]{2,1,0:T(8,128)S(1)} fusion(bf16[96,128,256]{2,1,0:T(8,128)(2,1)} %gather_fusion, bf16[288,128,128]{2,1,0:T(8,128)(2,1)} %get-tuple-element.262, s32[]{:T(128)S(6)} %select_n.56), kind=kOutput, calls=%fused_computation.7.clone.1 | convolution fusion | flops 805306368 | bytes 22020100 | tf_op jit(solution)/shard_map/while/body/tij,tjd->tid/dot_general | solution.py:71
  92.8 13.7 %fusion.62 = f32[24,128,256]{2,0,1:T(8,128)S(1)} fusion(f32[24,128,256]{2,0,1:T(8,128)S(1)} %copy-done.4, f32[96,128,256]{2,1,0:T(8,128)S(1)} %fusion.61, f32[96]{0:T(128)S(1)} %compare_convert_fusion.4, s32[96]{0:T(128)S(1)} %dynamic_slice.32), kind=kOutput, calls=%fused_computation.9.clone.1 | convolution fusion | flops 906760704 | bytes 18875136 | tf_op jit(solution)/shard_map/while/body/tr,tid->rid/dot_general | solution.py:77
  113.0 2.3 multiply_convert_fusion
  119.2 5.6 %fusion.31 = bf16[3072,256]{1,0:T(8,128)(2,1)S(1)} fusion(bf16[256,256]{1,0:T(8,128)(2,1)S(1)} %copy-done.10, f32[3072,256]{1,0:T(8,128)} %copy-done.13, bf16[3072,256]{1,0:T(8,128)(2,1)S(1)} %copy-done.9), kind=kOutput, calls=%fused_computation.42 | convolution fusion | flops 421527552 | bytes 6422528 | tf_op jit(solution)/shard_map/dot_general | solution.py:97
  124.8 3.5 broadcast_in_dim.13
  128.3 30.3 %while.21 = (s32[]{:T(128)}, f32[48,128,256]{2,0,1:T(8,128)}, s32[]{:T(128)}, s32[288]{0:T(512)S(1)}, s32[]{:T(128)}, /*index=5*/bf16[288,128,128]{2,1,0:T(8,128...) while((s32[]{:T(128)}, f32[48,128,256]{2,0,1:T(8,128)}, ...), condition=%wide.region_3.4_spmd, body=%wide.region_2.3_spmd.sunk | while | flops 2618829312 | bytes 110108272 | solution.py:117
  129.3 6.0 %gather_fusion.1 = bf16[96,128,256]{2,1,0:T(8,128)(2,1)} fusion(bf16[24,128,256]{2,1,0:T(8,128)(2,1)S(1)} %get-tuple-element.300, s32[1024]{0:T(1024)S(1)} %pad_clamp_fusion.6), kind=kCustom, calls=%fused_computation.1.clone.1 | custom fusion | bytes 12583296 | tf_op jit(solution)/shard_map/while/body/gather | solution.py:108
  135.2 5.7 %fusion.67 = f32[96,128,256]{2,1,0:T(8,128)S(1)} fusion(bf16[96,128,256]{2,1,0:T(8,128)(2,1)} %gather_fusion.1, bf16[288,128,128]{2,1,0:T(8,128)(2,1)} %get-tuple-element.298, s32[]{:T(128)S(6)} %select_n.58), kind=kOutput, calls=%fused_computation.23.clone.1 | convolution fusion | flops 805306368 | bytes 22020100 | tf_op jit(solution)/shard_map/while/body/tji,tjd->tid/dot_general | solution.py:107
  141.0 14.8 %fusion.68 = f32[48,128,256]{2,0,1:T(8,128)S(1)} fusion(f32[48,128,256]{2,0,1:T(8,128)S(1)} %copy-done.2, f32[96,128,256]{2,1,0:T(8,128)S(1)} %fusion.67, f32[96]{0:T(128)S(1)} %compare_convert_fusion.5, s32[96]{0:T(128)S(1)} %dynamic_slice.35), kind=kOutput, calls=%fused_computation.25.clone.1 | convolution fusion | flops 1813521408 | bytes 25166592 | tf_op jit(solution)/shard_map/while/body/tc,tid->cid/dot_general | solution.py:113
  155.8 2.7 copy-done.3
  158.6 6.1 %copy.29 = bf16[48,128,256]{2,1,0:T(8,128)(2,1)S(1)} copy(f32[48,128,256]{2,0,1:T(8,128)} %get-tuple-element.90) | data formatting | bytes 9437184 | tf_op jit(solution)/shard_map/while | solution.py:117
  165.6 123.2 %all-to-all-start.3 = ((bf16[128,8,256]{2,1,0:T(8,128)(2,1)}), bf16[128,8,256]{2,1,0:T(8,128)(2,1)S(1)}, u32[]{:S(2)}, u32[]{:S(2)}) async-start(bf16[128,8,256]{2,1,0:T(8,128)(2,1)} %bitcast.15), calls=%async_computation.3 | async-start | bytes 1048576 | tf_op jit(solution)/shard_map/all_to_all | solution.py:130
  291.6 2.6 copy.28
  294.3 83.0 %all-reduce.5.cloned.1.call-done = f32[256,256]{1,0:T(8,128)} async-done(((f32[256,256]{1,0:T(8,128)}), f32[256,256]{1,0:T(8,128)}) %all-reduce.5.cloned.1.call-update) | async-done | bytes 262160 | tf_op jit(solution)/shard_map/psum | solution.py:133
  378.9 9.7 %scatter_custom_fusion = f32[3072,256]{1,0:T(8,128)} fusion(f32[3072,256]{1,0:T(8,128)} %bitcast.48, s32[1024]{0:T(1024)} %bitcast.51, bf16[128,8,256]{2,1,0:T(8,128)(2,1)S(1)} %all-to-all-done.3), kind=kCustom, calls=%fused_computation.50 | custom fusion | flops 524288 | bytes 3670016 | tf_op jit(solution)/shard_map/scatter-add | solution.py:132
  (61 shorter events, 24.7 us)
Async XLA Ops:
  7.2 27.2 %copy-start = (bf16[3072,256]{1,0:T(8,128)(2,1)S(1)}, bf16[3072,256]{1,0:T(8,128)(2,1)}, u32[]{:S(2)}) copy-start(bf16[3072,256]{1,0:T(8,128)(2,1)} %param.17) | copy-start | bytes 4718596
  8.6 14.5 %all-to-all-start.1 = ((s32[8,1,2]{2,1,0:T(1,128)}), s32[8,1,2]{2,1,0:T(1,128)S(1)}, u32[]{:S(2)}, u32[]{:S(2)}) async-start(s32[8,1,2]{2,1,0:T(1,128)} %copy.25), calls=%async_computation.1 | async-start | bytes 8192 | tf_op jit(solution)/shard_map/all_to_all | solution.py:50
  16.4 0.6 copy-start.8
  23.2 42.9 %copy-start.6 = (bf16[3072,256]{1,0:T(8,128)(2,1)S(1)}, bf16[3072,256]{1,0:T(8,128)(2,1)}, u32[]{:S(2)}) copy-start(bf16[3072,256]{1,0:T(8,128)(2,1)} %param.15) | copy-start | bytes 4718596
  23.2 22.9 %all-to-all-start = ((bf16[128,8,256]{2,1,0:T(8,128)(2,1)}), bf16[128,8,256]{2,1,0:T(8,128)(2,1)}, u32[]{:S(2)}, u32[]{:S(2)}) async-start(bf16[128,8,256]{2,1,0:T(8,128)(2,1)} %bitcast.49), calls=%async_computation | async-start | bytes 1048576 | tf_op jit(solution)/shard_map/all_to_all | solution.py:48
  46.1 19.9 %all-to-all-start.2 = ((bf16[8,256,256]{2,1,0:T(8,128)(2,1)}), bf16[8,256,256]{2,1,0:T(8,128)(2,1)S(1)}, u32[]{:S(2)}, u32[]{:S(2)}) async-start(bf16[8,256,256]{2,1,0:T(8,128)(2,1)} %bitcast.46), calls=%async_computation.2 | async-start | bytes 2097152 | tf_op jit(solution)/shard_map/all_to_all | solution.py:53
  50.9 237.9 %all-reduce.3.cloned.1.call-start = ((), (), s32[]{:S(2)}) async-start(), calls=%async_computation.4 | async-start | bytes 524288 | tf_op jit(solution)/shard_map/psum | solution.py:133
  76.3 1.9 copy-start.11
  76.3 1.9 copy-start.12
  87.1 5.7 %copy-start.4 = (f32[24,128,256]{2,0,1:T(8,128)S(1)}, f32[24,128,256]{2,0,1:T(8,128)}, u32[]{:S(2)}) copy-start(f32[24,128,256]{2,0,1:T(8,128)} %get-tuple-element.246) | copy-start | bytes 9437188 | tf_op jit(solution)/shard_map/while
  106.5 1.7 copy-start.5
  110.7 1.4 copy-start.7
  112.1 0.9 copy-start.10
  113.0 4.0 %copy-start.9 = (bf16[3072,256]{1,0:T(8,128)(2,1)S(1)}, bf16[3072,256]{1,0:T(8,128)(2,1)}, u32[]{:S(2)}) copy-start(bf16[3072,256]{1,0:T(8,128)(2,1)} %param.18) | copy-start | bytes 4718596
  115.3 1.7 copy-start.13
  135.2 5.7 %copy-start.2 = (f32[48,128,256]{2,0,1:T(8,128)S(1)}, f32[48,128,256]{2,0,1:T(8,128)}, u32[]{:S(2)}) copy-start(f32[48,128,256]{2,0,1:T(8,128)} %get-tuple-element.282) | copy-start | bytes 18874372 | tf_op jit(solution)/shard_map/while
  155.8 2.7 copy-start.3
  165.6 213.4 %all-to-all-start.3 = ((bf16[128,8,256]{2,1,0:T(8,128)(2,1)}), bf16[128,8,256]{2,1,0:T(8,128)(2,1)S(1)}, u32[]{:S(2)}, u32[]{:S(2)}) async-start(bf16[128,8,256]{2,1,0:T(8,128)(2,1)} %bitcast.15), calls=%async_computation.3 | async-start | bytes 1048576 | tf_op jit(solution)/shard_map/all_to_all | solution.py:130
  288.7 88.5 %all-reduce.5.cloned.1.call-start = ((), (), s32[]{:S(2)}) async-start(), calls=%async_computation.5 | async-start | bytes 524288 | tf_op jit(solution)/shard_map/psum | solution.py:133
  291.6 97.1 %copy-start.1 = (bf16[3072,256]{1,0:T(8,128)(2,1)S(1)}, bf16[3072,256]{1,0:T(8,128)(2,1)}, u32[]{:S(2)}) copy-start(bf16[3072,256]{1,0:T(8,128)(2,1)} %param.17) | copy-start | bytes 4718596
Sparse Core Ops, SparseCore 0:
  125.0 112.8 all-reduce.2
  293.1 84.1 all-reduce.4
